TPU v7x, 32 devices: a whole 2x2x4 slice. The times are simulated.
32 devices in a mesh: expert: 16 (over z, y, core), dp: 2 (over x).
Axes of the slice: x: 2, y: 2, z: 4, core: 2. Of those that a mesh axis runs over, the one named last changes fastest.
Arguments:
- tokens: bfloat16 [4096, 2048], P(('expert', 'dp')), may hold values from -6 to 6
- targets: bfloat16 [4096, 2048], P(('expert', 'dp')), may hold values from -6 to 6
- router: bfloat16 [2048, 16], replicated, may hold values from -0.125 to 0.125
- picks: int32 [4096, 16, 4], P(('expert', 'dp')), may hold values from 0 to 1, as said below
- w_gate_up: bfloat16 [16, 2, 1408, 2048], P('expert', None, 'dp'), may hold values from -0.125 to 0.125
- w_down: bfloat16 [16, 1408, 2048], P('expert', 'dp'), may hold values from -0.15625 to 0.15625
- v_gate_up: bfloat16 [16, 2, 1408, 2048], P('expert', None, 'dp'), may hold values from -0.125 to 0.125
- v_down: bfloat16 [16, 1408, 2048], P('expert', 'dp'), may hold values from -0.15625 to 0.15625
Outputs:
- mixed: bfloat16 [4096, 2048], P(('expert', 'dp'))
- hvp_gate_up: float32 [16, 2, 1408, 2048], P('expert', None, 'dp')
- hvp_down: float32 [16, 1408, 2048], P('expert', 'dp')
Inputs may be any that keep to these rules, and one draw needn't show every extreme that they name: In every block of 128 tokens (one device's rows), for each expert e and slot c exactly one token t has picks[t, e, c] = 1, and an expert never picks a token twice.
All inputs are finite; a program needn't handle non-finite values.
Results may differ from a plain program's by a relative error of at most 0.009.
Values may be sent and summed in bfloat16 or wider, within the bound.
A program may use at most 128 MiB of HBM per device.

v0:
```python
import math

import jax
import jax.numpy as jnp
from jax import lax
from jax.sharding import PartitionSpec as P


def regroup(block, lead):
    count, total, width = block.shape
    parted = block.reshape(count, lead, total // lead, width)
    return jnp.swapaxes(parted, 0, 1).reshape(lead, count * total // lead, width)


def local(tokens, targets, router, picks, w_gate_up, w_down, v_gate_up, v_down):
    highest = lax.Precision.HIGHEST
    n_exp = lax.axis_size("expert")
    exp_dev = w_down.shape[0]
    onehot = picks.astype(jnp.bfloat16)
    gates = jax.nn.sigmoid(jnp.dot(tokens, router, preferred_element_type=jnp.float32))
    outgoing = jnp.einsum("tec,td->ecd", onehot, tokens, preferred_element_type=jnp.float32).astype(
        jnp.bfloat16
    )
    arrived = lax.all_to_all(outgoing, "expert", split_axis=0, concat_axis=0, tiled=True)
    rows = lax.all_gather(regroup(arrived, exp_dev), "dp", axis=1, tiled=True)
    scale = 1.0 / math.sqrt(rows.shape[1])
    primal = jnp.einsum("ekfd,erd->ekfr", w_gate_up, rows, preferred_element_type=jnp.float32)
    tangent = jnp.einsum("ekfd,erd->ekfr", v_gate_up, rows, preferred_element_type=jnp.float32)
    gate_pre, up_pre = (primal[:, 0], primal[:, 1])
    gate_dot, up_dot = (tangent[:, 0], tangent[:, 1])
    sigma = jax.nn.sigmoid(gate_pre)
    active = gate_pre * sigma
    slope = sigma * (1.0 + gate_pre * (1.0 - sigma))
    curve = sigma * (1.0 - sigma) * (2.0 + gate_pre * (1.0 - 2.0 * sigma))
    act_dot = slope * gate_dot
    hidden = (active * up_pre).astype(jnp.bfloat16)
    hidden_dot = (act_dot * up_pre + active * up_dot).astype(jnp.bfloat16)
    part_out = jnp.einsum("efr,efd->erd", hidden, w_down, preferred_element_type=jnp.float32)
    part_dot = jnp.einsum(
        "efr,efd->erd", hidden_dot, w_down, preferred_element_type=jnp.float32
    ) + jnp.einsum("efr,efd->erd", hidden, v_down, preferred_element_type=jnp.float32)
    own_out, own_dot = (
        lax.psum_scatter(part_out, "dp", scatter_dimension=1, tiled=True),
        lax.psum_scatter(part_dot, "dp", scatter_dimension=1, tiled=True),
    )
    back_out = regroup(own_out.astype(jnp.bfloat16), n_exp)
    back_dot = regroup(own_dot.astype(jnp.bfloat16), n_exp)
    ret_out, ret_dot = (
        lax.all_to_all(back_out, "expert", split_axis=0, concat_axis=0, tiled=True),
        lax.all_to_all(back_dot, "expert", split_axis=0, concat_axis=0, tiled=True),
    )
    ret_out = ret_out.astype(jnp.float32)
    ret_dot = ret_dot.astype(jnp.float32)
    weighted = picks.astype(jnp.float32) * gates[:, :, None]
    combined = jnp.einsum("tec,ecd->td", weighted, ret_out, precision=highest)
    combined_dot = jnp.einsum("tec,ecd->td", weighted, ret_dot, precision=highest)
    mixed = combined.astype(jnp.bfloat16)
    resid = scale * (combined - targets.astype(jnp.float32))
    resid_dot = scale * combined_dot
    cot_send = jnp.einsum("tec,td->ecd", weighted, resid, precision=highest).astype(jnp.bfloat16)
    cdot_send = jnp.einsum("tec,td->ecd", weighted, resid_dot, precision=highest).astype(
        jnp.bfloat16
    )
    cot_got, cdot_got = (
        lax.all_to_all(cot_send, "expert", split_axis=0, concat_axis=0, tiled=True),
        lax.all_to_all(cdot_send, "expert", split_axis=0, concat_axis=0, tiled=True),
    )
    own_cot = regroup(cot_got, exp_dev)
    own_cdot = regroup(cdot_got, exp_dev)
    cot_rows, cdot_rows = (
        lax.all_gather(own_cot, "dp", axis=1, tiled=True),
        lax.all_gather(own_cdot, "dp", axis=1, tiled=True),
    )
    grad_hid = jnp.einsum("erd,efd->efr", cot_rows, w_down, preferred_element_type=jnp.float32)
    grad_hdot = jnp.einsum(
        "erd,efd->efr", cdot_rows, w_down, preferred_element_type=jnp.float32
    ) + jnp.einsum("erd,efd->efr", cot_rows, v_down, preferred_element_type=jnp.float32)
    hvp_down = jnp.einsum(
        "efr,erd->efd", hidden_dot, cot_rows, preferred_element_type=jnp.float32
    ) + jnp.einsum("efr,erd->efd", hidden, cdot_rows, preferred_element_type=jnp.float32)
    gate_term = (
        (grad_hdot * up_pre + grad_hid * up_dot) * slope + grad_hid * up_pre * curve * gate_dot
    ).astype(jnp.bfloat16)
    up_term = (grad_hdot * active + grad_hid * act_dot).astype(jnp.bfloat16)
    both_terms = jnp.stack([gate_term, up_term], axis=1)
    hvp_gate_up = jnp.einsum("ekfr,erd->ekfd", both_terms, rows, preferred_element_type=jnp.float32)
    return (mixed, hvp_gate_up, hvp_down)


def solution(mesh):
    placed = (
        P(("expert", "dp"), None),
        P(("expert", "dp"), None),
        P(),
        P(("expert", "dp"), None, None),
        P("expert", None, "dp", None),
        P("expert", "dp", None),
        P("expert", None, "dp", None),
        P("expert", "dp", None),
    )
    return jax.shard_map(
        local,
        mesh=mesh,
        in_specs=placed,
        out_specs=(
            P(("expert", "dp"), None),
            P("expert", None, "dp", None),
            P("expert", "dp", None),
        ),
        check_vma=False,
    )
```

profile of v0, /device:TPU:0, one launch (start us, length us, event | category | flops | bytes accessed | tf_op | source)
XLA Modules:
  0.0 175.9 jit_solution(7330747647602827392)
XLA Ops:
  7.2 0.0 copy-start
  7.2 0.0 reduce-scatter.3.cloned.1.call-start
  7.2 0.9 convert_element_type.62
  8.1 1.3 convolution_convert_fusion.2
  9.4 0.2 copy.35
  9.6 17.2 %all_to_all.25 = bf16[16,4,2048]{2,1,0:T(4,128)(2,1)S(1)} all-to-all(bf16[16,4,2048]{2,1,0:T(4,128)(2,1)S(1)} %copy.35), channel_id=1, replica_groups=mesh['expert'=16,'dp'=2] {'expert'}, dimensions={0} | all-to-all | bytes 524288 | tf_op jit(solution)/shard_map/all_to_all | solution.py:24
  26.9 0.8 reshape_transpose_reshape.15
  27.6 8.9 %all_gather.9 = bf16[1,128,2048]{2,1,0:T(8,128)(2,1)S(1)} all-gather(bf16[1,64,2048]{2,1,0:T(8,128)(2,1)} %reshape_transpose_reshape.15), channel_id=1, replica_groups=mesh['expert'=16,'dp'=2] {'dp'}, dimensions={1}, use_global_device_ids=true | all-gather | bytes 786432 | tf_op jit(solution)/shard_map/all_gather | solution.py:25
  36.6 4.5 %fusion.30 = f32[1,2,704,128]{3,2,1,0:T(8,128)S(1)} fusion(bf16[1,2,704,2048]{3,2,1,0:T(8,128)(2,1)} %param.14, bf16[1,128,2048]{2,1,0:T(8,128)(2,1)S(1)} %all_gather.9), kind=kOutput, calls=%fused_computation.29 | convolution fusion | flops 738197504 | bytes 7012352 | tf_op jit(solution)/shard_map/ekfd,erd->ekfr/dot_general | solution.py:28
  41.0 0.0 copy-done.2
  41.0 0.0 copy-start.7
  41.1 1.7 fusion.27
  42.7 0.0 copy-done.7
  42.7 0.0 copy-start.9
  42.7 1.0 add_convert_fusion
  43.7 0.0 copy-done.9
  43.7 0.7 copy-done.5
  44.4 0.0 copy-done
  44.4 1.6 fusion.22
  46.0 0.0 reduce-scatter.3.cloned.1.call-update
  46.0 0.0 reduce-scatter.5.cloned.1.call-start
  46.0 0.0 copy-start.11
  46.1 2.6 %fusion.6 = f32[128,2048]{1,0:T(8,128)S(1)} fusion(bf16[704,128]{1,0:T(8,128)(2,1)} %copy-done.5, bf16[1,704,2048]{2,1,0:T(8,128)(2,1)} %param.15), kind=kOutput, calls=%fused_computation.8 | convolution fusion | flops 369098752 | bytes 4112384 | tf_op jit(solution)/shard_map/efr,efd->erd/dot_general | solution.py:41
  48.6 0.0 copy-done.11
  48.6 0.0 copy-start.14
  48.6 1.6 fusion.19
  50.2 0.0 reduce-scatter.5.cloned.1.call-update
  50.3 14.8 %reduce-scatter.3.cloned.1.call-done = f32[1,64,2048]{2,1,0:T(8,128)} async-done(((f32[1,128,2048]{2,1,0:T(8,128)}), f32[1,64,2048]{2,1,0:T(8,128)}) %reduce-scatter.3.cloned.1.call-update) | async-done | bytes 524304 | tf_op jit(solution)/shard_map/reduce_scatter | solution.py:43
  65.1 1.8 %convert_element_type.66 = bf16[1,64,2048]{2,1,0:T(8,128)(2,1)} convert(f32[1,64,2048]{2,1,0:T(8,128)} %reduce-scatter.3.cloned.1.call-done) | non-fusion elementwise | flops 131072 | bytes 786432 | tf_op jit(solution)/shard_map/convert_element_type | solution.py:46
  66.8 1.8 reshape_transpose_reshape.16
  68.6 5.7 %all-to-all-start.1 = ((bf16[16,4,2048]{2,1,0:T(4,128)(2,1)}), bf16[16,4,2048]{2,1,0:T(4,128)(2,1)}, u32[]{:S(2)}, u32[]{:S(2)}) async-start(bf16[16,4,2048]{2,1,0:T(4,128)(2,1)} %reshape_transpose_reshape.16), calls=%async_computation.2 | async-start | bytes 524288 | tf_op jit(solution)/shard_map/all_to_all | solution.py:49
  74.3 0.0 copy-done.14
  74.3 1.3 fusion.44
  75.6 0.0 copy-done.13
  75.6 12.7 %reduce-scatter.5.cloned.1.call-done = f32[1,64,2048]{2,1,0:T(8,128)} async-done(((f32[1,128,2048]{2,1,0:T(8,128)}), f32[1,64,2048]{2,1,0:T(8,128)}) %reduce-scatter.5.cloned.1.call-update) | async-done | bytes 524304 | tf_op jit(solution)/shard_map/reduce_scatter | solution.py:44
  88.3 1.8 %convert_element_type.70 = bf16[1,64,2048]{2,1,0:T(8,128)(2,1)} convert(f32[1,64,2048]{2,1,0:T(8,128)} %reduce-scatter.5.cloned.1.call-done) | non-fusion elementwise | flops 131072 | bytes 786432 | tf_op jit(solution)/shard_map/convert_element_type | solution.py:47
  90.1 1.8 reshape_transpose_reshape.17
  91.9 0.0 all-to-all-done.1
  91.9 5.7 %all-to-all-start.2 = ((bf16[16,4,2048]{2,1,0:T(4,128)(2,1)}), bf16[16,4,2048]{2,1,0:T(4,128)(2,1)}, u32[]{:S(2)}, u32[]{:S(2)}) async-start(bf16[16,4,2048]{2,1,0:T(4,128)(2,1)} %reshape_transpose_reshape.17), calls=%async_computation.4 | async-start | bytes 524288 | tf_op jit(solution)/shard_map/all_to_all | solution.py:50
  97.5 2.4 %fusion.94 = (bf16[128,2048]{1,0:T(8,128)(2,1)}, f32[128,2048]{1,0:T(8,128)S(1)}) fusion(bf16[16,4,2048]{2,1,0:T(4,128)(2,1)} %all-to-all-done.1, f32[128,16,4]{0,2,1:T(4,128)S(1)} %convert_multiply_fusion), kind=kOutput, calls=%fused_computation.100 | convolution fusion | flops 201588736 | bytes 1867776 | tf_op jit(solution)/shard_map/tec,ecd->td/dot_general | solution.py:55
  99.9 1.8 %convolution_convert_fusion = bf16[16,4,2048]{2,0,1:T(8,128)(2,1)S(1)} fusion(f32[128,2048]{1,0:T(8,128)S(1)} %get-tuple-element.8, bf16[128,2048]{1,0:T(8,128)(2,1)} %param.9, f32[128,16,4]{0,2,1:T(4,128)S(1)} %convert_multiply_fusion), kind=kOutput, calls=%fused_computation.25 | convolution fusion | flops 202244096 | bytes 1867776 | tf_op jit(solution)/shard_map/tec,td->ecd/dot_general | solution.py:60
  101.7 0.9 copy.43
  102.7 5.0 %all-to-all-done.2 = bf16[16,4,2048]{2,1,0:T(4,128)(2,1)} async-done(((bf16[16,4,2048]{2,1,0:T(4,128)(2,1)}), bf16[16,4,2048]{2,1,0:T(4,128)(2,1)}, u32[]{:S(2)}, u32[]{:S(2)}) %all-to-all-start.2) | async-done | bytes 262176 | tf_op jit(solution)/shard_map/all_to_all | solution.py:50
  107.6 4.2 %all-to-all-start.4 = ((bf16[16,4,2048]{2,1,0:T(4,128)(2,1)}), bf16[16,4,2048]{2,1,0:T(4,128)(2,1)}, u32[]{:S(2)}, u32[]{:S(2)}) async-start(bf16[16,4,2048]{2,1,0:T(4,128)(2,1)} %copy.43), calls=%async_computation.6 | async-start | bytes 524288 | tf_op jit(solution)/shard_map/all_to_all | solution.py:65
  111.8 1.6 fusion.26
  113.4 0.7 convolution_convert_fusion.1
  114.1 0.9 copy.41
  115.0 6.9 %all-to-all-done.4 = bf16[16,4,2048]{2,1,0:T(4,128)(2,1)} async-done(((bf16[16,4,2048]{2,1,0:T(4,128)(2,1)}), bf16[16,4,2048]{2,1,0:T(4,128)(2,1)}, u32[]{:S(2)}, u32[]{:S(2)}) %all-to-all-start.4) | async-done | bytes 262176 | tf_op jit(solution)/shard_map/all_to_all | solution.py:65
  121.9 4.2 %all-to-all-start.3 = ((bf16[16,4,2048]{2,1,0:T(4,128)(2,1)}), bf16[16,4,2048]{2,1,0:T(4,128)(2,1)}, u32[]{:S(2)}, u32[]{:S(2)}) async-start(bf16[16,4,2048]{2,1,0:T(4,128)(2,1)} %copy.41), calls=%async_computation.5 | async-start | bytes 524288 | tf_op jit(solution)/shard_map/all_to_all | solution.py:66
  126.1 1.7 reshape_transpose_reshape.19
  127.8 9.6 %all_gather.11 = bf16[1,128,2048]{2,1,0:T(8,128)(2,1)S(1)} all-gather(bf16[1,64,2048]{2,1,0:T(8,128)(2,1)} %reshape_transpose_reshape.19), channel_id=1, replica_groups=mesh['expert'=16,'dp'=2] {'dp'}, dimensions={1}, use_global_device_ids=true | all-gather | bytes 786432 | tf_op jit(solution)/shard_map/all_gather | solution.py:71
  137.4 3.7 %fusion.4 = f32[128,704]{0,1:T(8,128)} fusion(bf16[1,704,2048]{2,1,0:T(8,128)(2,1)} %param.15, bf16[1,128,2048]{2,1,0:T(8,128)(2,1)S(1)} %all_gather.11), kind=kOutput, calls=%fused_computation.6 | convolution fusion | flops 369098752 | bytes 3768320 | tf_op jit(solution)/shard_map/erd,efd->efr/dot_general | solution.py:77
  141.1 0.0 copy-done.3
  141.1 0.0 copy-done.12
  141.1 3.4 %fusion.49 = f32[704,2048]{1,0:T(8,128)} fusion(bf16[1,128,2048]{2,1,0:T(8,128)(2,1)S(1)} %all_gather.11, bf16[1,1,704,128]{3,2,1,0:T(8,128)(2,1)S(1)} %copy-done.12), kind=kOutput, calls=%fused_computation.41 | convolution fusion | flops 369098752 | bytes 6471680 | tf_op jit(solution)/shard_map/efr,erd->efd/dot_general | solution.py:78
  144.6 0.0 all-to-all-done.3
  144.6 1.7 reshape_transpose_reshape.18
  146.3 8.6 %all_gather.10 = bf16[1,128,2048]{2,1,0:T(8,128)(2,1)S(1)} all-gather(bf16[1,64,2048]{2,1,0:T(8,128)(2,1)} %reshape_transpose_reshape.18), channel_id=1, replica_groups=mesh['expert'=16,'dp'=2] {'dp'}, dimensions={1}, use_global_device_ids=true | all-gather | bytes 786432 | tf_op jit(solution)/shard_map/all_gather | solution.py:72
  154.9 1.9 %fusion.36 = f32[704,128]{1,0:T(8,128)S(1)} fusion(f32[128,704]{0,1:T(8,128)} %fusion.4, bf16[1,704,2048]{2,1,0:T(8,128)(2,1)S(1)} %copy-done, bf16[1,128,2048]{2,1,0:T(8,128)(2,1)S(1)} %all_gather.10), kind=kOutput, calls=%fused_computation.31 | convolution fusion | flops 369188864 | bytes 4128768 | tf_op jit(solution)/shard_map/erd,efd->efr/dot_general | solution.py:75
  156.9 0.0 copy-start.1
  156.9 1.1 fusion.86
  158.0 1.5 copy-done.1
  159.5 3.4 %add_bitcast_fusion = f32[1,704,2048]{2,1,0:T(8,128)} fusion(f32[704,2048]{1,0:T(8,128)S(1)} %copy-done.1, bf16[704,128]{1,0:T(8,128)(2,1)S(1)} %copy-done.6, bf16[1,128,2048]{2,1,0:T(8,128)(2,1)S(1)} %all_gather.10), kind=kOutput, calls=%fused_computation.4 | convolution fusion | flops 370540544 | bytes 12238848 | tf_op jit(solution)/shard_map/efr,erd->efd/dot_general | solution.py:80
  162.9 6.1 %convolution_bitcast_fusion = f32[1,2,704,2048]{3,2,1,0:T(8,128)} fusion(bf16[1,128,2048]{2,1,0:T(8,128)(2,1)S(1)} %all_gather.9, bf16[1,1,704,128]{3,2,1,0:T(8,128)(2,1)S(1)} %get-tuple-element.4, bf16[1,1,704,128]{3,2,1,0:T(8,128)(2,1)S(1)} %get-tuple-element.3), kind=kOutput, calls=%fused_computation.5 | convolution fusion | flops 738377728 | bytes 12419072 | tf_op jit(solution)/shard_map/ekfr,erd->ekfd/dot_general | solution.py:86
  (14 shorter events, 0.0 us)
Async XLA Ops:
  7.2 37.2 %copy-start = (bf16[1,704,2048]{2,1,0:T(8,128)(2,1)S(1)}, bf16[1,704,2048]{2,1,0:T(8,128)(2,1)}, u32[]{:S(2)}) copy-start(bf16[1,704,2048]{2,1,0:T(8,128)(2,1)} %param.13) | copy-start | bytes 8650756
  7.2 57.9 %reduce-scatter.3.cloned.1.call-start = ((), (), s32[]{:S(2)}) async-start(), calls=%async_computation.7 | async-start | bytes 1572864 | tf_op jit(solution)/shard_map/reduce_scatter | solution.py:43
  36.6 4.5 %copy-start.2 = (bf16[1,2,704,2048]{3,2,1,0:T(8,128)(2,1)S(1)}, bf16[1,2,704,2048]{3,2,1,0:T(8,128)(2,1)}, u32[]{:S(2)}) copy-start(bf16[1,2,704,2048]{3,2,1,0:T(8,128)(2,1)} %param.12) | copy-start | bytes 17301508
  41.0 1.7 copy-start.7
  42.7 1.0 copy-start.9
  43.7 0.7 copy-start.5
  46.0 42.3 %reduce-scatter.5.cloned.1.call-start = ((), (), s32[]{:S(2)}) async-start(), calls=%async_computation.8 | async-start | bytes 1572864 | tf_op jit(solution)/shard_map/reduce_scatter | solution.py:44
  46.0 2.6 %copy-start.11 = (bf16[1,1,704,128]{3,2,1,0:T(8,128)(2,1)S(1)}, bf16[1,1,704,128]{3,2,1,0:T(8,128)(2,1)}, u32[]{:S(2)}) copy-start(bf16[1,1,704,128]{3,2,1,0:T(8,128)(2,1)} %get-tuple-element.5) | copy-start | bytes 540676
  48.6 25.6 %copy-start.14 = (bf16[2048,16]{0,1:T(8,128)(2,1)S(1)}, bf16[2048,16]{0,1:T(8,128)(2,1)}, u32[]{:S(2)}) copy-start(bf16[2048,16]{0,1:T(8,128)(2,1)} %param.10) | copy-start | bytes 196612
  50.2 25.4 %copy-start.13 = (s32[128,16,4]{0,2,1:T(4,128)S(1)}, s32[128,16,4]{0,2,1:T(4,128)}, u32[]{:S(2)}) copy-start(s32[128,16,4]{0,2,1:T(4,128)} %param.11) | copy-start | bytes 98308
  68.6 23.3 %all-to-all-start.1 = ((bf16[16,4,2048]{2,1,0:T(4,128)(2,1)}), bf16[16,4,2048]{2,1,0:T(4,128)(2,1)}, u32[]{:S(2)}, u32[]{:S(2)}) async-start(bf16[16,4,2048]{2,1,0:T(4,128)(2,1)} %reshape_transpose_reshape.16), calls=%async_computation.2 | async-start | bytes 524288 | tf_op jit(solution)/shard_map/all_to_all | solution.py:49
  91.9 15.8 %all-to-all-start.2 = ((bf16[16,4,2048]{2,1,0:T(4,128)(2,1)}), bf16[16,4,2048]{2,1,0:T(4,128)(2,1)}, u32[]{:S(2)}, u32[]{:S(2)}) async-start(bf16[16,4,2048]{2,1,0:T(4,128)(2,1)} %reshape_transpose_reshape.17), calls=%async_computation.4 | async-start | bytes 524288 | tf_op jit(solution)/shard_map/all_to_all | solution.py:50
  107.6 14.3 %all-to-all-start.4 = ((bf16[16,4,2048]{2,1,0:T(4,128)(2,1)}), bf16[16,4,2048]{2,1,0:T(4,128)(2,1)}, u32[]{:S(2)}, u32[]{:S(2)}) async-start(bf16[16,4,2048]{2,1,0:T(4,128)(2,1)} %copy.43), calls=%async_computation.6 | async-start | bytes 524288 | tf_op jit(solution)/shard_map/all_to_all | solution.py:65
  121.9 22.7 %all-to-all-start.3 = ((bf16[16,4,2048]{2,1,0:T(4,128)(2,1)}), bf16[16,4,2048]{2,1,0:T(4,128)(2,1)}, u32[]{:S(2)}, u32[]{:S(2)}) async-start(bf16[16,4,2048]{2,1,0:T(4,128)(2,1)} %copy.41), calls=%async_computation.5 | async-start | bytes 524288 | tf_op jit(solution)/shard_map/all_to_all | solution.py:66
  127.8 13.3 %copy-start.12 = (bf16[1,1,704,128]{3,2,1,0:T(8,128)(2,1)S(1)}, bf16[1,1,704,128]{3,2,1,0:T(8,128)(2,1)}, u32[]{:S(2)}) copy-start(bf16[1,1,704,128]{3,2,1,0:T(8,128)(2,1)} %get-tuple-element.5) | copy-start | bytes 540676
  137.4 3.7 %copy-start.3 = (bf16[1,128,2048]{2,1,0:T(8,128)(2,1)}, bf16[1,128,2048]{2,1,0:T(8,128)(2,1)S(1)}, u32[]{:S(2)}) copy-start(bf16[1,128,2048]{2,1,0:T(8,128)(2,1)S(1)} %all_gather.11) | copy-start | bytes 1572868
  146.3 10.6 %copy-start.4 = (bf16[1,128,2048]{2,1,0:T(8,128)(2,1)S(1)}, bf16[1,128,2048]{2,1,0:T(8,128)(2,1)}, u32[]{:S(2)}) copy-start(bf16[1,128,2048]{2,1,0:T(8,128)(2,1)} %copy-done.3) | copy-start | bytes 1572868
  146.3 10.6 %copy-start.8 = (f32[1,2,704,128]{3,2,1,0:T(8,128)S(1)}, f32[1,2,704,128]{3,2,1,0:T(8,128)}, u32[]{:S(2)}) copy-start(f32[1,2,704,128]{3,2,1,0:T(8,128)} %copy-done.7) | copy-start | bytes 2162692
  146.3 10.6 %copy-start.10 = (f32[1,2,704,128]{3,2,1,0:T(8,128)S(1)}, f32[1,2,704,128]{3,2,1,0:T(8,128)}, u32[]{:S(2)}) copy-start(f32[1,2,704,128]{3,2,1,0:T(8,128)} %copy-done.9) | copy-start | bytes 2162692
  156.9 2.6 %copy-start.1 = (f32[704,2048]{1,0:T(8,128)S(1)}, f32[704,2048]{1,0:T(8,128)}, u32[]{:S(2)}) copy-start(f32[704,2048]{1,0:T(8,128)} %fusion.49) | copy-start | bytes 17301508
  156.9 2.6 %copy-start.6 = (bf16[704,128]{1,0:T(8,128)(2,1)S(1)}, bf16[704,128]{1,0:T(8,128)(2,1)}, u32[]{:S(2)}) copy-start(bf16[704,128]{1,0:T(8,128)(2,1)} %copy-done.5) | copy-start | bytes 540676
Sparse Core Ops, SparseCore 0:
  46.1 18.9 reduce-scatter.2
  68.0 20.3 reduce-scatter.4
where the time goes:
time: 177 us; the launch traced here: 176 us
  blocking collectives  44.4 us (25%)
  matrix products  40.6 us (23%)
  waiting for transfers between devices  39.4 us (22%)
  starting transfers between devices  19.8 us (11%)
  between operations  14.3 us (8%)
  local copies, waits for them, and re-layouts  11.9 us (7%)
  other arithmetic  5.42 us (3%)
    all_to_all x1, blocking collectives, local(): lax.all_to_all(outgoing, 'expert', split_axis=0, concat_axis=0, tiled=True)  17.2 us
    reduce_scatter x1, waiting for transfers between devices, local(): lax.psum_scatter(part_out, 'dp', scatter_dimension=1, tiled=True)  14.8 us
    reduce_scatter x1, waiting for transfers between devices, local(): lax.psum_scatter(part_dot, 'dp', scatter_dimension=1, tiled=True)  12.7 us
    all_gather x1, blocking collectives, local(): lax.all_gather(own_cot, 'dp', axis=1, tiled=True)  9.63 us
    all_gather x1, blocking collectives, local(): rows = lax.all_gather(regroup(arrived, exp_dev), 'dp', axis=1, tiled=True)  8.94 us
    all_gather x1, blocking collectives, local(): lax.all_gather(own_cdot, 'dp', axis=1, tiled=True)  8.63 us
    another operation x5, local copies, waits for them, and re-layouts, regroup(): jnp.swapaxes(parted, 0, 1).reshape(lead, count * total // lead, width)  7.71 us
    all_to_all x1, waiting for transfers between devices, local(): lax.all_to_all(cot_send, 'expert', split_axis=0, concat_axis=0, tiled=True)  6.87 us
  transfers between devices with their start and end apart: 6, of which 4 were waited for; matrix products, arithmetic and copies ran while one was open for 17% of the time, Pallas kernels for 0%

commit v1 on v0

--- a/solution.py
+++ b/solution.py
@@ -1,8 +1,11 @@
+import functools
 import math
 
 import jax
 import jax.numpy as jnp
 from jax import lax
+from jax.experimental import pallas as pl
+from jax.experimental.pallas import tpu as pltpu
 from jax.sharding import PartitionSpec as P
 
 
@@ -87,7 +90,346 @@
     return (mixed, hvp_gate_up, hvp_down)
 
 
+f32, bf16 = jnp.float32, jnp.bfloat16
+NT = (((1,), (1,)), ((), ()))
+TN = (((0,), (0,)), ((), ()))
+PIECES = 4
+
+
+def mm(a, b, dims=(((1,), (0,)), ((), ()))):
+    return lax.dot_general(a, b, dims, preferred_element_type=f32)
+
+
+def iota2(shape, dim):
+    return lax.broadcasted_iota(jnp.int32, shape, dim)
+
+
+def main_kernel(
+    n_exp, ff, width,
+    tok, tgt, router, onehot, wgu_hbm, wd_hbm, vgu_hbm, vd_hbm,
+    mixed, rows, hh, cc, terms,
+    wgu, vgu, wd, vd,
+    send, recv, ret_send, ret_recv, xsend, xrecv, own, hht, keep, gstack, btk, gcol,
+    wsem, ssem, rsem, fs_sem, fr_sem, xs_sem, xr_sem,
+):
+    me = lax.axis_index("expert")
+    peer = 1 - lax.axis_index("dp")
+    piece = width // PIECES
+    half = n_exp * 4
+    blocks = n_exp * 16
+    scale = 1.0 / math.sqrt(2 * half)
+
+    loads = [
+        pltpu.make_async_copy(src, dst, wsem.at[i])
+        for i, (src, dst) in enumerate(
+            [(wgu_hbm, wgu), (vgu_hbm, vgu), (wd_hbm, wd), (vd_hbm, vd)]
+        )
+    ]
+    for load in loads:
+        load.start()
+
+    barrier = pltpu.get_barrier_semaphore()
+
+    @pl.loop(1, n_exp)
+    def _(k):
+        pl.semaphore_signal(
+            barrier, inc=1, device_id={"expert": lax.rem(me + k, n_exp)},
+            device_id_type=pl.DeviceIdType.MESH,
+        )
+
+    pl.semaphore_signal(barrier, inc=1, device_id={"dp": peer}, device_id_type=pl.DeviceIdType.MESH)
+
+    def hop(t, k, src, dst):
+        to = lax.rem(me + k, n_exp)
+        return pltpu.make_async_remote_copy(
+            src_ref=src.at[to], dst_ref=dst.at[me], send_sem=ssem.at[t, k], recv_sem=rsem.at[t, k],
+            device_id={"expert": to}, device_id_type=pl.DeviceIdType.MESH,
+        )
+
+    def arrival(t, k, src, dst):
+        come = lax.rem(me + n_exp - k, n_exp)
+        return pltpu.make_async_remote_copy(
+            src_ref=src.at[come], dst_ref=dst.at[come], send_sem=ssem.at[t, k],
+            recv_sem=rsem.at[t, k], device_id={"expert": come}, device_id_type=pl.DeviceIdType.MESH,
+        )
+
+    def relay(t, k, buf):
+        come = lax.rem(me + n_exp - k, n_exp)
+        return pltpu.make_async_remote_copy(
+            src_ref=buf.at[0, come], dst_ref=buf.at[1, come], send_sem=fs_sem.at[t, k],
+            recv_sem=fr_sem.at[t, k], device_id={"dp": peer}, device_id_type=pl.DeviceIdType.MESH,
+        )
+
+    def cross(t, p):
+        return pltpu.make_async_remote_copy(
+            src_ref=xsend.at[t, p], dst_ref=xrecv.at[t, p], send_sem=xs_sem.at[t, p],
+            recv_sem=xr_sem.at[t, p], device_id={"dp": peer}, device_id_type=pl.DeviceIdType.MESH,
+        )
+
+    def spread(t, src, dst):
+        @pl.loop(1, n_exp)
+        def _(k):
+            hop(t, k, src, dst).start()
+
+        dst[me] = src[me]
+
+    row_b, col_b = iota2((blocks, half), 0), iota2((blocks, half), 1)
+    all_pieces = jnp.where(
+        ((row_b >> 4) == (col_b >> 2)) & ((row_b & 3) == (col_b & 3)), 1.0, 0.0
+    ).astype(bf16)
+    picked_t = mm(all_pieces, onehot[...], NT)
+    row_t = iota2(picked_t.shape, 0)
+    for p in range(PIECES):
+        btk[:, p * 128 : (p + 1) * 128] = jnp.where(
+            ((row_t >> 2) & 3) == p, picked_t, 0.0
+        ).astype(bf16)
+    stacked = jnp.concatenate([tok[:, p * piece : (p + 1) * piece] for p in range(PIECES)], axis=0)
+    send[0] = mm(btk[...], stacked).astype(bf16).reshape(n_exp, 16, piece)
+    pl.semaphore_wait(barrier, n_exp)
+    spread(0, send.at[0], recv.at[0, 0])
+    relay(0, 0, recv.at[0]).start()
+
+    gates = jax.nn.sigmoid(mm(tok[...], router[...]))
+    g_hi = gates.astype(bf16)
+    g_lo = (gates - g_hi.astype(f32)).astype(bf16)
+    lane_e, col_e = iota2((n_exp, blocks), 0), iota2((n_exp, blocks), 1)
+    widen = jnp.where(lane_e == (col_e >> 4), 1.0, 0.0).astype(bf16)
+    weight = mm(onehot[...], all_pieces, NT) * (mm(g_hi, widen) + mm(g_lo, widen))
+    w_hi = weight.astype(bf16).astype(f32)
+    w_lo = weight - w_hi
+    col_w = iota2(weight.shape, 1)
+    for p in range(PIECES):
+        at_piece = ((col_w >> 2) & 3) == p
+        gstack[p * 256 : p * 256 + 128] = jnp.where(at_piece, w_hi, 0.0).astype(bf16)
+        gstack[p * 256 + 128 : p * 256 + 256] = jnp.where(at_piece, w_lo, 0.0).astype(bf16)
+    by_expert = mm(picked_t.astype(bf16), g_hi) + mm(picked_t.astype(bf16), g_lo)
+    own_lane = (iota2(by_expert.shape, 0) >> 4) == iota2(by_expert.shape, 1)
+    gcol[...] = jnp.broadcast_to(
+        jnp.sum(jnp.where(own_lane, by_expert, 0.0), axis=1, keepdims=True), gcol.shape
+    )
+
+
+    def to_rows_matrix():
+        rr, cp = iota2((blocks, blocks), 0), iota2((blocks, blocks), 1)
+        inside = lax.rem(rr, half)
+        want = (inside >> 2) * 16 + lax.div(rr, half) * 4 + (inside & 3)
+        return jnp.where(cp == want, 1.0, 0.0).astype(bf16)
+
+    perm = to_rows_matrix()
+
+    def unpack(buf, dst, row0):
+        flat = mm(perm, buf[...].reshape(blocks, piece)).astype(bf16)
+        for p in range(PIECES):
+            dst[row0 : row0 + half, p * piece : (p + 1) * piece] = flat[p * half : (p + 1) * half]
+
+    def receive_and_relay(t, a, src, buf):
+        @pl.loop(1, n_exp)
+        def _(k):
+            arrival(a, k, src, buf.at[0]).wait_recv()
+            relay(t, k, buf).start()
+
+    def relays_in(t, buf):
+        @pl.loop(0, n_exp)
+        def _(k):
+            relay(t, k, buf).wait_recv()
+
+    receive_and_relay(0, 0, send.at[0], recv.at[0])
+    unpack(recv.at[0, 0], rows, 0)
+    relays_in(0, recv.at[0])
+    unpack(recv.at[0, 1], rows, half)
+
+    loads[0].wait()
+    loads[1].wait()
+    tile = ff // 2
+
+    @pl.loop(0, 2)
+    def _(i):
+        at = pl.ds(pl.multiple_of(i * tile, tile), tile)
+        gate_pre = mm(wgu[0, at], rows[...], NT)
+        up_pre = mm(wgu[1, at], rows[...], NT)
+        gate_dot = mm(vgu[0, at], rows[...], NT)
+        up_dot = mm(vgu[1, at], rows[...], NT)
+        sigma = jax.nn.sigmoid(gate_pre)
+        active = gate_pre * sigma
+        slope = sigma * (1.0 + gate_pre * (1.0 - sigma))
+        curve = sigma * (1.0 - sigma) * (2.0 + gate_pre * (1.0 - 2.0 * sigma))
+        act_dot = slope * gate_dot
+        hh[at, :128] = (act_dot * up_pre + active * up_dot).astype(bf16)
+        hh[at, 128:] = (active * up_pre).astype(bf16)
+        keep[0, at] = up_pre * slope
+        keep[1, at] = up_dot * slope + up_pre * curve * gate_dot
+        keep[2, at] = active
+        keep[3, at] = act_dot
+
+    hht[...] = jnp.transpose(hh[...])
+    loads[2].wait()
+    loads[3].wait()
+    hid_t = hht[128:]
+    for p in range(PIECES):
+        cols = slice(p * piece, (p + 1) * piece)
+        part = mm(hid_t, wd[:, cols])
+        own[0, p] = part[:half]
+        xsend[0, p] = part[half:].astype(bf16)
+        cross(0, p).start()
+    for p in range(PIECES):
+        cols = slice(p * piece, (p + 1) * piece)
+        part = mm(hht[:128], wd[:, cols]) + mm(hid_t, vd[:, cols])
+        own[1, p] = part[:half]
+        xsend[1, p] = part[half:].astype(bf16)
+        cross(1, p).start()
+    for t in range(2):
+        for p in range(PIECES):
+            cross(t, p).wait_recv()
+        total = (own[t] + xrecv[t].astype(f32)).astype(bf16).reshape(blocks, piece)
+        ret_send[t] = mm(perm, total, TN).astype(bf16).reshape(n_exp, 16, piece)
+        spread(1 + t, ret_send.at[t], ret_recv.at[t])
+
+    for t in range(2):
+        @pl.loop(1, n_exp)
+        def _(k):
+            arrival(1 + t, k, ret_send.at[t], ret_recv.at[t]).wait_recv()
+
+        got = ret_recv[t].reshape(blocks, piece)
+        his, los = [], []
+        for p in range(PIECES):
+            cols = slice(p * piece, (p + 1) * piece)
+            both = mm(gstack[p * 256 : (p + 1) * 256], got)
+            comb = both[:128] + both[128:]
+            if t == 0:
+                mixed[:, cols] = comb.astype(bf16)
+                resid = scale * (comb - tgt[:, cols].astype(f32))
+            else:
+                resid = scale * comb
+            hi = resid.astype(bf16)
+            his.append(hi)
+            los.append((resid - hi.astype(f32)).astype(bf16))
+        taken = mm(btk[...], jnp.concatenate(his, axis=0)) + mm(
+            btk[...], jnp.concatenate(los, axis=0)
+        )
+        send[1 + t] = (taken * gcol[:, :1]).astype(bf16).reshape(n_exp, 16, piece)
+        spread(3 + t, send.at[1 + t], recv.at[1 + t, 0])
+        relay(1 + t, 0, recv.at[1 + t]).start()
+
+    for t in range(2):
+        receive_and_relay(1 + t, 3 + t, send.at[1 + t], recv.at[1 + t])
+        unpack(recv.at[1 + t, 0], cc, t * 128)
+    for t in range(2):
+        relays_in(1 + t, recv.at[1 + t])
+        unpack(recv.at[1 + t, 1], cc, t * 128 + half)
+
+    @pl.loop(0, 2)
+    def _(i):
+        at = pl.ds(pl.multiple_of(i * tile, tile), tile)
+        grads = mm(wd[at], cc[...], NT)
+        grad_hid = grads[:, :128]
+        grad_hdot = grads[:, 128:] + mm(vd[at], cc[:128], NT)
+        terms[0, at] = (grad_hdot * keep[0, at] + grad_hid * keep[1, at]).astype(bf16)
+        terms[1, at] = (grad_hdot * keep[2, at] + grad_hid * keep[3, at]).astype(bf16)
+
+    @pl.loop(1, n_exp)
+    def _(k):
+        for t in range(3):
+            hop((0, 3, 4)[t], k, send.at[t], recv.at[t, 0]).wait_send()
+        for t in range(2):
+            hop(1 + t, k, ret_send.at[t], ret_recv.at[t]).wait_send()
+
+    @pl.loop(0, n_exp)
+    def _(k):
+        for t in range(3):
+            relay(t, k, recv.at[t]).wait_send()
+
+    for t in range(2):
+        for p in range(PIECES):
+            cross(t, p).wait_send()
+
+
+def out_kernel(terms, rows, hh, cc, gu, down):
+    gu[0, 0] = mm(terms[0], rows[...])
+    gu[0, 1] = mm(terms[1], rows[...])
+    down[0] = mm(hh[...], cc[...])
+
+
+def fused(n_exp, n_dp, tokens, targets, router, picks, w_gate_up, w_down, v_gate_up, v_down):
+    toks, width = tokens.shape
+    ff = w_down.shape[1]
+    piece = width // PIECES
+    half = n_exp * 4
+    blocks = n_exp * 16
+    onehot = picks.reshape(toks, half).astype(bf16)
+    vmem = pl.BlockSpec(memory_space=pltpu.VMEM)
+    hbm = pl.BlockSpec(memory_space=pl.ANY)
+    dma = pltpu.SemaphoreType.DMA
+    mixed, rows, hh, cc, terms = pl.pallas_call(
+        functools.partial(main_kernel, n_exp, ff, width),
+        out_shape=(
+            jax.ShapeDtypeStruct((toks, width), bf16),
+            jax.ShapeDtypeStruct((2 * half, width), bf16),
+            jax.ShapeDtypeStruct((ff, 256), bf16),
+            jax.ShapeDtypeStruct((4 * half, width), bf16),
+            jax.ShapeDtypeStruct((2, ff, 128), bf16),
+        ),
+        in_specs=[vmem] * 4 + [hbm] * 4,
+        out_specs=(vmem,) * 5,
+        scratch_shapes=[
+            pltpu.VMEM((2, ff, width), bf16),
+            pltpu.VMEM((2, ff, width), bf16),
+            pltpu.VMEM((ff, width), bf16),
+            pltpu.VMEM((ff, width), bf16),
+            pltpu.VMEM((3, n_exp, 16, piece), bf16),
+            pltpu.VMEM((3, 2, n_exp, 16, piece), bf16),
+            pltpu.VMEM((2, n_exp, 16, piece), bf16),
+            pltpu.VMEM((2, n_exp, 16, piece), bf16),
+            pltpu.VMEM((2, PIECES, half, piece), bf16),
+            pltpu.VMEM((2, PIECES, half, piece), bf16),
+            pltpu.VMEM((2, PIECES, half, piece), f32),
+            pltpu.VMEM((256, ff), bf16),
+            pltpu.VMEM((4, ff, 128), f32),
+            pltpu.VMEM((PIECES * 256, blocks), bf16),
+            pltpu.VMEM((blocks, PIECES * 128), bf16),
+            pltpu.VMEM((blocks, 128), f32),
+            dma((4,)),
+            dma((5, n_exp)),
+            dma((5, n_exp)),
+            dma((3, n_exp)),
+            dma((3, n_exp)),
+            dma((2, PIECES)),
+            dma((2, PIECES)),
+        ],
+        compiler_params=pltpu.CompilerParams(
+            collective_id=0, has_side_effects=True, vmem_limit_bytes=56 * 2**20
+        ),
+        cost_estimate=pl.CostEstimate(
+            flops=20 * 128 * ff * width, bytes_accessed=12 * ff * width, transcendentals=ff * 128
+        ),
+        name="experts",
+    )(tokens, targets, router, onehot, w_gate_up[0], w_down[0], v_gate_up[0], v_down[0])
+    tile = ff // 4
+    hvp_gate_up, hvp_down = pl.pallas_call(
+        out_kernel,
+        grid=(4,),
+        out_shape=(
+            jax.ShapeDtypeStruct((1, 2, ff, width), f32),
+            jax.ShapeDtypeStruct((1, ff, width), f32),
+        ),
+        in_specs=[
+            pl.BlockSpec((2, tile, 128), lambda i: (0, i, 0)),
+            pl.BlockSpec((2 * half, width), lambda i: (0, 0)),
+            pl.BlockSpec((tile, 256), lambda i: (i, 0)),
+            pl.BlockSpec((4 * half, width), lambda i: (0, 0)),
+        ],
+        out_specs=(
+            pl.BlockSpec((1, 2, tile, width), lambda i: (0, 0, i, 0)),
+            pl.BlockSpec((1, tile, width), lambda i: (0, i, 0)),
+        ),
+        compiler_params=pltpu.CompilerParams(vmem_limit_bytes=48 * 2**20),
+        name="products",
+    )(terms, rows, hh, cc)
+    return mixed, hvp_gate_up, hvp_down
+
+
 def solution(mesh):
+    n_exp, n_dp = mesh.shape["expert"], mesh.shape["dp"]
+    small = n_dp == 2 and n_exp <= 16
     placed = (
         P(("expert", "dp"), None),
         P(("expert", "dp"), None),
@@ -99,7 +441,7 @@
         P("expert", "dp", None),
     )
     return jax.shard_map(
-        local,
+        functools.partial(fused, n_exp, n_dp) if small else local,
         mesh=mesh,
         in_specs=placed,
         out_specs=(

time: 177 us -> 81.9 us (0.46)
  Pallas kernels: 0 us -> 71.3 us
  blocking collectives: 44.4 us -> 0 us
  matrix products: 40.6 us -> 0 us
  waiting for transfers between devices: 39.4 us -> 0 us
  starting transfers between devices: 19.8 us -> 0 us
  between operations: 14.3 us -> 0.65 us
  other arithmetic: 5.42 us -> 0.77 us
  local copies, waits for them, and re-layouts: 11.9 us -> 8.67 us
    pallas_call x0 -> x2, Pallas kernels: none -> 71.3 us  [the longest x1 64.5 us: fused(): pl.pallas_call(functools.partial(main_kernel, n_exp, ff, width), out_shap...]
    dot_general x17 -> x0, matrix products: 40.6 us -> none  [the longest x1 6.08 us: local(): jnp.einsum('ekfr,erd->ekfd', both_terms, rows, preferred_element_type=jnp...]
    reduce_scatter x2 -> x0, waiting for transfers between devices: 27.5 us -> none  [the longest x1 14.8 us: local(): lax.psum_scatter(part_out, 'dp', scatter_dimension=1, tiled=True)]
    all_gather x3 -> x0, blocking collectives: 27.2 us -> none  [the longest x1 9.63 us: local(): lax.all_gather(own_cot, 'dp', axis=1, tiled=True)]
    all_to_all x4 -> x0, starting transfers between devices: 19.7 us -> none  [the longest x1 5.67 us: local(): lax.all_to_all(back_dot, 'expert', split_axis=0, concat_axis=0, tiled=True)]
    all_to_all x1 -> x0, blocking collectives: 17.2 us -> none  [local(): lax.all_to_all(outgoing, 'expert', split_axis=0, concat_axis=0, tiled=True)]
    all_to_all x4 -> x0, waiting for transfers between devices: 11.9 us -> none  [the longest x1 6.87 us: local(): lax.all_to_all(cot_send, 'expert', split_axis=0, concat_axis=0, tiled=True)]
    another operation x5 -> x0, local copies, waits for them, and re-layouts: 7.71 us -> none  [regroup(): jnp.swapaxes(parted, 0, 1).reshape(lead, count * total // lead, width)]
  transfers between devices with their start and end apart: 6 -> 0, of which waited for: 4 -> 0; matrix products, arithmetic and copies ran while one was open for 17% -> 0% of each run, Pallas kernels for 0% -> 0%
where the time goes in v1:
time: 81.9 us; the launch traced here: 81.4 us
  Pallas kernels  71.3 us (87%)
  local copies, waits for them, and re-layouts  8.67 us (11%)
    pallas_call x1, Pallas kernels, fused(): pl.pallas_call(functools.partial(main_kernel, n_exp, ff, width), out_shap...  64.5 us
    unnamed x10, local copies, waits for them, and re-layouts  7.95 us
    pallas_call x1, Pallas kernels, fused(): pl.pallas_call(out_kernel, grid=(4,), out_shape=(jax.ShapeDtypeStruct((1,...  6.8 us

profile of v1, /device:TPU:0, one launch (start us, length us, event | category | flops | bytes accessed | tf_op | source)
XLA Modules:
  0.0 81.4 jit_solution(17702961741394538502)
XLA Ops:
  0.6 0.8 convert_element_type.5
  1.4 0.7 copy.14.onehot
  2.1 1.8 %copy.13.router = bf16[2048,16]{1,0:T(8,128)(2,1)} copy(bf16[2048,16]{0,1:T(8,128)(2,1)} %param.10) | data formatting | bytes 131072 | tf_op args[2]
  4.0 64.5 %experts.1 = (bf16[128,2048]{1,0:T(8,128)(2,1)}, bf16[128,2048]{1,0:T(8,128)(2,1)}, bf16[704,256]{1,0:T(8,128)(2,1)}, bf16[256,2048]{1,0:T(8,128)(2,1)}, bf16[2,704,128]{2,1,0:T(8,128)(2,1)}) custom-call(bf16[128,2048]{1,0:T(8,128)(2,1)} %tok.1, bf16[128,2048]{1,0:T(8,128)(2,1)} %tgt.1, bf16[2048,16]{1,0:T(8,128)(2,1)} %copy.13.router, ...), custom_call_target="tpu_custom_call" | custom-call | flops 3690987520 | bytes 17301504 | tf_op jit(solution)/shard_map/experts/pallas_call | solution.py:362
  68.5 0.0 copy-start
  68.5 1.2 %copy-done = bf16[256,2048]{1,0:T(8,128)(2,1)S(1)} copy-done((bf16[256,2048]{1,0:T(8,128)(2,1)S(1)}, bf16[256,2048]{1,0:T(8,128)(2,1)}, u32[]{:S(2)}) %copy-start) | copy-done | bytes 1048600
  69.7 0.0 copy-start.1
  69.7 1.0 %copy-done.1 = bf16[128,2048]{1,0:T(8,128)(2,1)S(1)} copy-done((bf16[128,2048]{1,0:T(8,128)(2,1)S(1)}, bf16[128,2048]{1,0:T(8,128)(2,1)}, u32[]{:S(2)}) %copy-start.1) | copy-done | bytes 524312
  70.8 0.0 copy-start.2
  70.8 1.0 %copy-done.2 = bf16[704,256]{1,0:T(8,128)(2,1)S(1)} copy-done((bf16[704,256]{1,0:T(8,128)(2,1)S(1)}, bf16[704,256]{1,0:T(8,128)(2,1)}, u32[]{:S(2)}) %copy-start.2) | copy-done | bytes 360472
  71.7 0.0 copy-start.3
  71.7 1.0 %copy-done.3 = bf16[2,704,128]{2,1,0:T(8,128)(2,1)S(1)} copy-done((bf16[2,704,128]{2,1,0:T(8,128)(2,1)S(1)}, bf16[2,704,128]{2,1,0:T(8,128)(2,1)}, u32[]{:S(2)}) %copy-start.3) | copy-done | bytes 360472
  72.7 6.8 %products.1 = (f32[1,2,704,2048]{3,2,1,0:T(8,128)}, f32[1,704,2048]{2,1,0:T(8,128)}) custom-call(bf16[2,704,128]{2,1,0:T(8,128)(2,1)S(1)} %copy-done.3, bf16[128,2048]{1,0:T(8,128)(2,1)S(1)} %copy-done.1, bf16[704,256]{1,0:T(8,128)(2,1)S(1)} %copy-done.2, bf16[256,2048]{1,0:T(8,128)(2,1)S(1)} %copy-done), custom_call_target="tpu_custom_call" | custom-call | tf_op jit(solution)/shard_map/products/pallas_call | solution.py:407
  79.5 1.9 %copy.16 = bf16[128,2048]{1,0:T(8,128)(2,1)} copy(bf16[128,2048]{1,0:T(8,128)(2,1)} %get-tuple-element.20) | data formatting | bytes 1048576
Async XLA Ops:
  68.5 1.2 %copy-start = (bf16[256,2048]{1,0:T(8,128)(2,1)S(1)}, bf16[256,2048]{1,0:T(8,128)(2,1)}, u32[]{:S(2)}) copy-start(bf16[256,2048]{1,0:T(8,128)(2,1)} %get-tuple-element.14.cc) | copy-start | bytes 3145732
  69.7 1.0 %copy-start.1 = (bf16[128,2048]{1,0:T(8,128)(2,1)S(1)}, bf16[128,2048]{1,0:T(8,128)(2,1)}, u32[]{:S(2)}) copy-start(bf16[128,2048]{1,0:T(8,128)(2,1)} %get-tuple-element.12.rows) | copy-start | bytes 1572868
  70.8 1.0 %copy-start.2 = (bf16[704,256]{1,0:T(8,128)(2,1)S(1)}, bf16[704,256]{1,0:T(8,128)(2,1)}, u32[]{:S(2)}) copy-start(bf16[704,256]{1,0:T(8,128)(2,1)} %get-tuple-element.13.hh) | copy-start | bytes 1081348
  71.7 1.0 %copy-start.3 = (bf16[2,704,128]{2,1,0:T(8,128)(2,1)S(1)}, bf16[2,704,128]{2,1,0:T(8,128)(2,1)}, u32[]{:S(2)}) copy-start(bf16[2,704,128]{2,1,0:T(8,128)(2,1)} %get-tuple-element.11.terms) | copy-start | bytes 1081348

commit v2 on v1

--- a/solution.py
+++ b/solution.py
@@ -93,6 +93,7 @@
 f32, bf16 = jnp.float32, jnp.bfloat16
 NT = (((1,), (1,)), ((), ()))
 TN = (((0,), (0,)), ((), ()))
+ORDER = (2, 3, 1, 0)
 PIECES = 4
 
 
@@ -106,11 +107,12 @@
 
 def main_kernel(
     n_exp, ff, width,
-    tok, tgt, router, onehot, wgu_hbm, wd_hbm, vgu_hbm, vd_hbm,
-    mixed, rows, hh, cc, terms,
+    tok, tgt, router, picks, wgu_hbm, wd_hbm, vgu_hbm, vd_hbm,
+    mixed_out, rows_out, hh_out, cc_out, terms_out,
     wgu, vgu, wd, vd,
     send, recv, ret_send, ret_recv, xsend, xrecv, own, hht, keep, gstack, btk, gcol,
-    wsem, ssem, rsem, fs_sem, fr_sem, xs_sem, xr_sem,
+    mixed, rows, hh, cc, terms, chosen,
+    wsem, osem, ssem, rsem, fs_sem, fr_sem, xs_sem, xr_sem,
 ):
     me = lax.axis_index("expert")
     peer = 1 - lax.axis_index("dp")
@@ -139,45 +141,76 @@
 
     pl.semaphore_signal(barrier, inc=1, device_id={"dp": peer}, device_id_type=pl.DeviceIdType.MESH)
 
-    def hop(t, k, src, dst):
-        to = lax.rem(me + k, n_exp)
+    z, lane = lax.div(me, 4), lax.rem(me, 4)
+
+    def group(s):
+        if s == 0:
+            return z
+        if s == 1:
+            return z + 1 - 2 * lax.rem(z, 2)
+        if s == 2:
+            return lax.rem(z + 2, 4)
+        return 3 - z
+
+    def remote(src, dst, send_sem, recv_sem, **axis):
         return pltpu.make_async_remote_copy(
-            src_ref=src.at[to], dst_ref=dst.at[me], send_sem=ssem.at[t, k], recv_sem=rsem.at[t, k],
-            device_id={"expert": to}, device_id_type=pl.DeviceIdType.MESH,
+            src_ref=src, dst_ref=dst, send_sem=send_sem, recv_sem=recv_sem,
+            device_id=axis, device_id_type=pl.DeviceIdType.MESH,
         )
 
-    def arrival(t, k, src, dst):
-        come = lax.rem(me + n_exp - k, n_exp)
-        return pltpu.make_async_remote_copy(
-            src_ref=src.at[come], dst_ref=dst.at[come], send_sem=ssem.at[t, k],
-            recv_sem=rsem.at[t, k], device_id={"expert": come}, device_id_type=pl.DeviceIdType.MESH,
+    def four(s):
+        return pl.ds(group(s) * 4, 4)
+
+    def spread(t, s, src, dst):
+        if s == 0:
+            dst[me] = src[me]
+
+        @pl.loop(1 if s == 0 else 0, 4)
+        def _(j):
+            to = group(s) * 4 + lax.rem(lane + j, 4)
+            at = (t, 3 + j) if s == 0 else (t, s)
+            remote(src.at[to], dst.at[me], ssem.at[at], rsem.at[at], expert=to).start()
+
+    def arrived(t, s, dst):
+        if s == 0:
+            for j in range(1, 4):
+                come = z * 4 + lax.rem(lane + 4 - j, 4)
+                ref = dst.at[come]
+                remote(ref, ref, ssem.at[t, 3 + j], rsem.at[t, 3 + j], expert=come).wait_recv()
+        else:
+            ref = dst.at[four(s)]
+            remote(ref, ref, ssem.at[t, s], rsem.at[t, s], expert=group(s) * 4).wait_recv()
+
+    def sent(t, src):
+        for j in range(1, 4):
+            to = z * 4 + lax.rem(lane + j, 4)
+            ref = src.at[to]
+            remote(ref, ref, ssem.at[t, 3 + j], rsem.at[t, 3 + j], expert=to).wait_send()
+        for s in range(1, 4):
+            ref = src.at[four(s)]
+            remote(ref, ref, ssem.at[t, s], rsem.at[t, s], expert=group(s) * 4).wait_send()
+
+    def relay(t, s):
+        return remote(
+            recv.at[t, 0, four(s)], recv.at[t, 1, four(s)], fs_sem.at[t, s], fr_sem.at[t, s], dp=peer
         )
 
-    def relay(t, k, buf):
-        come = lax.rem(me + n_exp - k, n_exp)
-        return pltpu.make_async_remote_copy(
-            src_ref=buf.at[0, come], dst_ref=buf.at[1, come], send_sem=fs_sem.at[t, k],
-            recv_sem=fr_sem.at[t, k], device_id={"dp": peer}, device_id_type=pl.DeviceIdType.MESH,
-        )
-
-    def cross(t, p):
-        return pltpu.make_async_remote_copy(
-            src_ref=xsend.at[t, p], dst_ref=xrecv.at[t, p], send_sem=xs_sem.at[t, p],
-            recv_sem=xr_sem.at[t, p], device_id={"dp": peer}, device_id_type=pl.DeviceIdType.MESH,
-        )
-
-    def spread(t, src, dst):
-        @pl.loop(1, n_exp)
-        def _(k):
-            hop(t, k, src, dst).start()
-
-        dst[me] = src[me]
+    def cross(t, s):
+        g = group(s)
+        return remote(xsend.at[t, g], xrecv.at[t, g], xs_sem.at[t, s], xr_sem.at[t, s], dp=peer)
+
+    def write(i, src, dst):
+        copy = pltpu.make_async_copy(src, dst, osem.at[i])
+        copy.start()
+        return copy
 
     row_b, col_b = iota2((blocks, half), 0), iota2((blocks, half), 1)
     all_pieces = jnp.where(
         ((row_b >> 4) == (col_b >> 2)) & ((row_b & 3) == (col_b & 3)), 1.0, 0.0
     ).astype(bf16)
-    picked_t = mm(all_pieces, onehot[...], NT)
+    for e in range(n_exp):
+        chosen[e * 4 : e * 4 + 4] = picks[e].astype(f32)
+    picked_t = mm(all_pieces, chosen[...].astype(bf16))
     row_t = iota2(picked_t.shape, 0)
     for p in range(PIECES):
         btk[:, p * 128 : (p + 1) * 128] = jnp.where(
@@ -186,15 +219,15 @@
     stacked = jnp.concatenate([tok[:, p * piece : (p + 1) * piece] for p in range(PIECES)], axis=0)
     send[0] = mm(btk[...], stacked).astype(bf16).reshape(n_exp, 16, piece)
     pl.semaphore_wait(barrier, n_exp)
-    spread(0, send.at[0], recv.at[0, 0])
-    relay(0, 0, recv.at[0]).start()
-
-    gates = jax.nn.sigmoid(mm(tok[...], router[...]))
+    for s in ORDER:
+        spread(0, s, send.at[0], recv.at[0, 0])
+
+    gates = jax.nn.sigmoid(mm(tok[...], router[...], NT))
     g_hi = gates.astype(bf16)
     g_lo = (gates - g_hi.astype(f32)).astype(bf16)
     lane_e, col_e = iota2((n_exp, blocks), 0), iota2((n_exp, blocks), 1)
     widen = jnp.where(lane_e == (col_e >> 4), 1.0, 0.0).astype(bf16)
-    weight = mm(onehot[...], all_pieces, NT) * (mm(g_hi, widen) + mm(g_lo, widen))
+    weight = jnp.transpose(picked_t) * (mm(g_hi, widen) + mm(g_lo, widen))
     w_hi = weight.astype(bf16).astype(f32)
     w_lo = weight - w_hi
     col_w = iota2(weight.shape, 1)
@@ -222,21 +255,17 @@
         for p in range(PIECES):
             dst[row0 : row0 + half, p * piece : (p + 1) * piece] = flat[p * half : (p + 1) * half]
 
-    def receive_and_relay(t, a, src, buf):
-        @pl.loop(1, n_exp)
-        def _(k):
-            arrival(a, k, src, buf.at[0]).wait_recv()
-            relay(t, k, buf).start()
-
-    def relays_in(t, buf):
-        @pl.loop(0, n_exp)
-        def _(k):
-            relay(t, k, buf).wait_recv()
-
-    receive_and_relay(0, 0, send.at[0], recv.at[0])
+    def relay_in(t, a, s):
+        arrived(a, s, recv.at[t, 0])
+        relay(t, s).start()
+
+    for s in ORDER:
+        relay_in(0, 0, s)
     unpack(recv.at[0, 0], rows, 0)
-    relays_in(0, recv.at[0])
+    for s in ORDER:
+        relay(0, s).wait_recv()
     unpack(recv.at[0, 1], rows, half)
+    writes = [write(0, rows, rows_out)]
 
     loads[0].wait()
     loads[1].wait()
@@ -261,34 +290,39 @@
         keep[2, at] = active
         keep[3, at] = act_dot
 
+    writes.append(write(1, hh, hh_out))
     hht[...] = jnp.transpose(hh[...])
     loads[2].wait()
     loads[3].wait()
     hid_t = hht[128:]
-    for p in range(PIECES):
-        cols = slice(p * piece, (p + 1) * piece)
-        part = mm(hid_t, wd[:, cols])
-        own[0, p] = part[:half]
-        xsend[0, p] = part[half:].astype(bf16)
-        cross(0, p).start()
-    for p in range(PIECES):
-        cols = slice(p * piece, (p + 1) * piece)
-        part = mm(hht[:128], wd[:, cols]) + mm(hid_t, vd[:, cols])
-        own[1, p] = part[:half]
-        xsend[1, p] = part[half:].astype(bf16)
-        cross(1, p).start()
     for t in range(2):
         for p in range(PIECES):
-            cross(t, p).wait_recv()
-        total = (own[t] + xrecv[t].astype(f32)).astype(bf16).reshape(blocks, piece)
-        ret_send[t] = mm(perm, total, TN).astype(bf16).reshape(n_exp, 16, piece)
-        spread(1 + t, ret_send.at[t], ret_recv.at[t])
-
-    for t in range(2):
-        @pl.loop(1, n_exp)
-        def _(k):
-            arrival(1 + t, k, ret_send.at[t], ret_recv.at[t]).wait_recv()
-
+            cols = slice(p * piece, (p + 1) * piece)
+            if t == 0:
+                part = mm(hid_t, wd[:, cols])
+            else:
+                part = mm(hht[:128], wd[:, cols]) + mm(hid_t, vd[:, cols])
+            for g in range(4):
+                own[t, g, p] = part[g * 16 : g * 16 + 16]
+                xsend[t, g, p] = part[half + g * 16 : half + g * 16 + 16].astype(bf16)
+        for s in ORDER:
+            cross(t, s).start()
+
+    rq, cq = iota2((64, 64), 0), iota2((64, 64), 1)
+    perm_group = jnp.where(
+        cq == ((rq >> 2) & 3) * 16 + (rq >> 4) * 4 + (rq & 3), 1.0, 0.0
+    ).astype(bf16)
+
+    def give_back(t, s):
+        g = group(s)
+        cross(t, s).wait_recv()
+        total = (own[t, g] + xrecv[t, g].astype(f32)).astype(bf16).reshape(64, piece)
+        ret_send[t, four(s)] = mm(perm_group, total).astype(bf16).reshape(4, 16, piece)
+        spread(1 + t, s, ret_send.at[t], ret_recv.at[t])
+
+    def combine(t):
+        for s in ORDER:
+            arrived(1 + t, s, ret_recv.at[t])
         got = ret_recv[t].reshape(blocks, piece)
         his, los = [], []
         for p in range(PIECES):
@@ -307,43 +341,61 @@
             btk[...], jnp.concatenate(los, axis=0)
         )
         send[1 + t] = (taken * gcol[:, :1]).astype(bf16).reshape(n_exp, 16, piece)
-        spread(3 + t, send.at[1 + t], recv.at[1 + t, 0])
-        relay(1 + t, 0, recv.at[1 + t]).start()
-
+        for s in ORDER:
+            spread(3 + t, s, send.at[1 + t], recv.at[1 + t, 0])
+
+    for s in ORDER:
+        give_back(0, s)
+    for s in ORDER[:2]:
+        give_back(1, s)
+    combine(0)
+    writes.append(write(2, mixed, mixed_out))
+    for s in ORDER[2:]:
+        give_back(1, s)
+    for s in ORDER[:2]:
+        relay_in(1, 3, s)
+    combine(1)
+    for s in ORDER[2:]:
+        relay_in(1, 3, s)
+    unpack(recv.at[1, 0], cc, 0)
+    for s in ORDER:
+        relay(1, s).wait_recv()
+    unpack(recv.at[1, 1], cc, half)
+
+    tile = ff // 4
+    for i, s in enumerate(ORDER):
+        at = slice(i * tile, (i + 1) * tile)
+        grad_hid = mm(wd[at], cc[:128], NT)
+        grad_v = mm(vd[at], cc[:128], NT)
+        keep[1, at] = grad_hid * keep[1, at] + grad_v * keep[0, at]
+        keep[3, at] = grad_hid * keep[3, at] + grad_v * keep[2, at]
+        relay_in(2, 4, s)
+    unpack(recv.at[2, 0], cc, 128)
+    for s in ORDER:
+        relay(2, s).wait_recv()
+    unpack(recv.at[2, 1], cc, 128 + half)
+    writes.append(write(3, cc, cc_out))
+    for i in range(4):
+        at = slice(i * tile, (i + 1) * tile)
+        grad_c = mm(wd[at], cc[128:], NT)
+        terms[0, at] = (grad_c * keep[0, at] + keep[1, at]).astype(bf16)
+        terms[1, at] = (grad_c * keep[2, at] + keep[3, at]).astype(bf16)
+    writes.append(write(4, terms, terms_out))
+
+    for t in range(3):
+        sent((0, 3, 4)[t], send.at[t])
+        for s in ORDER:
+            relay(t, s).wait_send()
     for t in range(2):
-        receive_and_relay(1 + t, 3 + t, send.at[1 + t], recv.at[1 + t])
-        unpack(recv.at[1 + t, 0], cc, t * 128)
-    for t in range(2):
-        relays_in(1 + t, recv.at[1 + t])
-        unpack(recv.at[1 + t, 1], cc, t * 128 + half)
-
-    @pl.loop(0, 2)
-    def _(i):
-        at = pl.ds(pl.multiple_of(i * tile, tile), tile)
-        grads = mm(wd[at], cc[...], NT)
-        grad_hid = grads[:, :128]
-        grad_hdot = grads[:, 128:] + mm(vd[at], cc[:128], NT)
-        terms[0, at] = (grad_hdot * keep[0, at] + grad_hid * keep[1, at]).astype(bf16)
-        terms[1, at] = (grad_hdot * keep[2, at] + grad_hid * keep[3, at]).astype(bf16)
-
-    @pl.loop(1, n_exp)
-    def _(k):
-        for t in range(3):
-            hop((0, 3, 4)[t], k, send.at[t], recv.at[t, 0]).wait_send()
-        for t in range(2):
-            hop(1 + t, k, ret_send.at[t], ret_recv.at[t]).wait_send()
-
-    @pl.loop(0, n_exp)
-    def _(k):
-        for t in range(3):
-            relay(t, k, recv.at[t]).wait_send()
-
-    for t in range(2):
-        for p in range(PIECES):
-            cross(t, p).wait_send()
-
-
-def out_kernel(terms, rows, hh, cc, gu, down):
+        sent(1 + t, ret_send.at[t])
+        for s in ORDER:
+            cross(t, s).wait_send()
+    for copy in writes:
+        copy.wait()
+
+
+def out_kernel(terms, rows, hh, cc, mixed, gu, down, mixed_out):
+    mixed_out[...] = mixed[...]
     gu[0, 0] = mm(terms[0], rows[...])
     gu[0, 1] = mm(terms[1], rows[...])
     down[0] = mm(hh[...], cc[...])
@@ -355,7 +407,6 @@
     piece = width // PIECES
     half = n_exp * 4
     blocks = n_exp * 16
-    onehot = picks.reshape(toks, half).astype(bf16)
     vmem = pl.BlockSpec(memory_space=pltpu.VMEM)
     hbm = pl.BlockSpec(memory_space=pl.ANY)
     dma = pltpu.SemaphoreType.DMA
@@ -369,7 +420,7 @@
             jax.ShapeDtypeStruct((2, ff, 128), bf16),
         ),
         in_specs=[vmem] * 4 + [hbm] * 4,
-        out_specs=(vmem,) * 5,
+        out_specs=(hbm,) * 5,
         scratch_shapes=[
             pltpu.VMEM((2, ff, width), bf16),
             pltpu.VMEM((2, ff, width), bf16),
@@ -379,21 +430,28 @@
             pltpu.VMEM((3, 2, n_exp, 16, piece), bf16),
             pltpu.VMEM((2, n_exp, 16, piece), bf16),
             pltpu.VMEM((2, n_exp, 16, piece), bf16),
-            pltpu.VMEM((2, PIECES, half, piece), bf16),
-            pltpu.VMEM((2, PIECES, half, piece), bf16),
-            pltpu.VMEM((2, PIECES, half, piece), f32),
+            pltpu.VMEM((2, 4, PIECES, 16, piece), bf16),
+            pltpu.VMEM((2, 4, PIECES, 16, piece), bf16),
+            pltpu.VMEM((2, 4, PIECES, 16, piece), f32),
             pltpu.VMEM((256, ff), bf16),
             pltpu.VMEM((4, ff, 128), f32),
             pltpu.VMEM((PIECES * 256, blocks), bf16),
             pltpu.VMEM((blocks, PIECES * 128), bf16),
             pltpu.VMEM((blocks, 128), f32),
+            pltpu.VMEM((toks, width), bf16),
+            pltpu.VMEM((2 * half, width), bf16),
+            pltpu.VMEM((ff, 256), bf16),
+            pltpu.VMEM((4 * half, width), bf16),
+            pltpu.VMEM((2, ff, 128), bf16),
+            pltpu.VMEM((half, toks), f32),
             dma((4,)),
-            dma((5, n_exp)),
-            dma((5, n_exp)),
-            dma((3, n_exp)),
-            dma((3, n_exp)),
-            dma((2, PIECES)),
-            dma((2, PIECES)),
+            dma((5,)),
+            dma((5, 7)),
+            dma((5, 7)),
+            dma((3, 4)),
+            dma((3, 4)),
+            dma((2, 4)),
+            dma((2, 4)),
         ],
         compiler_params=pltpu.CompilerParams(
             collective_id=0, has_side_effects=True, vmem_limit_bytes=56 * 2**20
@@ -402,34 +460,37 @@
             flops=20 * 128 * ff * width, bytes_accessed=12 * ff * width, transcendentals=ff * 128
         ),
         name="experts",
-    )(tokens, targets, router, onehot, w_gate_up[0], w_down[0], v_gate_up[0], v_down[0])
+    )(tokens, targets, router.T, jnp.transpose(picks, (1, 2, 0)), w_gate_up[0], w_down[0], v_gate_up[0], v_down[0])
     tile = ff // 4
-    hvp_gate_up, hvp_down = pl.pallas_call(
+    hvp_gate_up, hvp_down, mixed = pl.pallas_call(
         out_kernel,
         grid=(4,),
         out_shape=(
             jax.ShapeDtypeStruct((1, 2, ff, width), f32),
             jax.ShapeDtypeStruct((1, ff, width), f32),
+            jax.ShapeDtypeStruct((toks, width), bf16),
         ),
         in_specs=[
             pl.BlockSpec((2, tile, 128), lambda i: (0, i, 0)),
             pl.BlockSpec((2 * half, width), lambda i: (0, 0)),
             pl.BlockSpec((tile, 256), lambda i: (i, 0)),
             pl.BlockSpec((4 * half, width), lambda i: (0, 0)),
+            pl.BlockSpec((toks // 4, width), lambda i: (i, 0)),
         ],
         out_specs=(
             pl.BlockSpec((1, 2, tile, width), lambda i: (0, 0, i, 0)),
             pl.BlockSpec((1, tile, width), lambda i: (0, i, 0)),
+            pl.BlockSpec((toks // 4, width), lambda i: (i, 0)),
         ),
-        compiler_params=pltpu.CompilerParams(vmem_limit_bytes=48 * 2**20),
+        compiler_params=pltpu.CompilerParams(vmem_limit_bytes=60 * 2**20),
         name="products",
-    )(terms, rows, hh, cc)
+    )(terms, rows, hh, cc, mixed)
     return mixed, hvp_gate_up, hvp_down
 
 
 def solution(mesh):
     n_exp, n_dp = mesh.shape["expert"], mesh.shape["dp"]
-    small = n_dp == 2 and n_exp <= 16
+    small = n_dp == 2 and n_exp == 16
     placed = (
         P(("expert", "dp"), None),
         P(("expert", "dp"), None),

time: 81.9 us -> 74.4 us (0.908)
  local copies, waits for them, and re-layouts: 8.67 us -> 0 us
  Pallas kernels: 71.3 us -> 73.6 us
    unnamed x10 -> x0, local copies, waits for them, and re-layouts: 7.95 us -> none
    pallas_call x1, Pallas kernels: 6.8 us -> 8.43 us  [fused(): pl.pallas_call(out_kernel, grid=(4,), out_shape=(jax.ShapeDtypeStruct((1,...]
where the time goes in v2:
time: 74.4 us; the launch traced here: 74.2 us
  Pallas kernels  73.6 us (99%)
    pallas_call x1, Pallas kernels, fused(): pl.pallas_call(functools.partial(main_kernel, n_exp, ff, width), out_shap...  65.1 us
    pallas_call x1, Pallas kernels, fused(): pl.pallas_call(out_kernel, grid=(4,), out_shape=(jax.ShapeDtypeStruct((1,...  8.43 us

profile of v2, /device:TPU:0, one launch (start us, length us, event | category | flops | bytes accessed | tf_op | source)
XLA Modules:
  0.0 74.2 jit_solution(2363461947242908669)
XLA Ops:
  0.6 65.1 %experts.1 = (bf16[128,2048]{1,0:T(8,128)(2,1)}, bf16[128,2048]{1,0:T(8,128)(2,1)}, bf16[704,256]{1,0:T(8,128)(2,1)}, bf16[256,2048]{1,0:T(8,128)(2,1)}, bf16[2,704,128]{2,1,0:T(8,128)(2,1)}) custom-call(bf16[128,2048]{1,0:T(8,128)(2,1)} %tok.1, bf16[128,2048]{1,0:T(8,128)(2,1)} %tgt.1, bf16[16,2048]{1,0:T(8,128)(2,1)} %bitcast.10, s32[16,4,128]{2,1,0:T(4,128)} %bitcast.11, ...), custom_call_target="tpu_custom_call" | custom-call | flops 3690987520 | bytes 17301504 | tf_op jit(solution)/shard_map/experts/pallas_call | solution.py:413
  65.8 8.4 %products.1 = (f32[1,2,704,2048]{3,2,1,0:T(8,128)}, f32[1,704,2048]{2,1,0:T(8,128)}, bf16[128,2048]{1,0:T(8,128)(2,1)}) custom-call(bf16[2,704,128]{2,1,0:T(8,128)(2,1)} %get-tuple-element.11.terms, bf16[128,2048]{1,0:T(8,128)(2,1)} %get-tuple-element.12.rows, bf16[704,256]{1,0:T(8,128)(2,1)} %get-tuple-element.13.hh, ...), custom_call_target="tpu_custom_call" | custom-call | tf_op jit(solution)/shard_map/products/pallas_call | solution.py:465
